TPU v7x, 256 devices: a whole 4x4x8 slice. The times are simulated.
256 devices in a mesh: ctx: 32 (over y_lo, z, core), fsdp: 8 (over y_hi, x).
Axes of the slice: x: 4, y: 4 (y_hi: 2, y_lo: 2; y = y_hi * 2 + y_lo), z: 8, core: 2. Of those that a mesh axis runs over, the one named last changes fastest.
Arguments:
- tokens: bfloat16 [12288, 5120], P('ctx', 'fsdp'), may hold values from -30 to 30
- tangents: bfloat16 [12288, 5120], P('ctx', 'fsdp'), may hold values from -6 to 6
- positions: int32 [12288], P('ctx'), may hold values from 0 to 12287, each once
- frames: int32 [12288], replicated, may hold values from 0 to 7, never falling along the last dimension, each value on 1 to 1560 neighbouring positions
- w_query: bfloat16 [5120, 3072], P('ctx', 'fsdp'), may hold values from -1 to 1
- w_key: bfloat16 [5120, 3072], P('ctx', 'fsdp'), may hold values from -1 to 1
- w_value: bfloat16 [5120, 3072], P('ctx', 'fsdp'), may hold values from -0.078125 to 0.078125
Outputs:
- attended: bfloat16 [12288, 3072], P('ctx', 'fsdp')
- attended_tangent: bfloat16 [12288, 3072], P('ctx', 'fsdp')
All inputs are finite; a program needn't handle non-finite values.
Results may differ from a plain program's by a relative error of at most 0.03.
Values may be sent and summed in bfloat16 or wider, within the bound.
A program may use at most 128 MiB of HBM per device.

v0:
```python
import jax
import jax.numpy as jnp
from jax import lax
from jax.sharding import PartitionSpec as P

DH = 128
SPAN = 4


def passed_along(block, axis, distance):
    devices = range(lax.axis_size(axis))
    route = [((i - distance) % len(devices), i) for i in devices]
    return lax.ppermute(block, axis, route)


def per_device(tokens, tangents, positions, frames, w_query, w_key, w_value):
    rows = tokens.shape[0]
    width = w_query.shape[1]
    local_heads = width // DH
    x_full, xt_full = (
        lax.all_gather(tokens, "fsdp", axis=1, tiled=True),
        lax.all_gather(tangents, "fsdp", axis=1, tiled=True),
    )
    stacked = jnp.concatenate([x_full, xt_full], 0)
    pieces = (
        lax.all_gather(w_query, "ctx", axis=0, tiled=True),
        lax.all_gather(w_key, "ctx", axis=0, tiled=True),
        lax.all_gather(w_value, "ctx", axis=0, tiled=True),
    )
    sums = tuple((jnp.dot(stacked, piece, preferred_element_type=jnp.float32) for piece in pieces))

    def split(made):
        made = made.astype(jnp.bfloat16)
        return (
            made[:rows].reshape(rows, local_heads, DH),
            made[rows:].reshape(rows, local_heads, DH),
        )

    query, query_t = split(sums[0])
    key, key_t = split(sums[1])
    value, value_t = split(sums[2])
    query_frames = jnp.take(frames, positions)
    earlier_frames = [query_frames]
    for step in range(1, SPAN + 1):
        earlier_frames.append(passed_along(query_frames, "ctx", step))
    scale = DH ** (-0.5)

    def update(state, block, block_frames):
        key_b, value_b, key_tb, value_tb = (block[0], block[1], block[2], block[3])
        allowed = block_frames[None, None, :] <= query_frames[None, :, None]
        score = jnp.einsum("qhd,khd->hqk", query, key_b, preferred_element_type=jnp.float32) * scale
        score_t = (
            jnp.einsum("qhd,khd->hqk", query_t, key_b, preferred_element_type=jnp.float32)
            + jnp.einsum("qhd,khd->hqk", query, key_tb, preferred_element_type=jnp.float32)
        ) * scale
        score = jnp.where(allowed, score, jnp.float32(-1e30))
        top_old, total, drift, plain, mixed, carried = state
        top_new = jnp.maximum(top_old, jnp.max(score, axis=2))
        shrink = jnp.exp(top_old - top_new)
        weight = jnp.where(allowed, jnp.exp(score - top_new[:, :, None]), jnp.float32(0.0))
        total = total * shrink + jnp.sum(weight, axis=2)
        drift = drift * shrink + jnp.sum(weight * score_t, axis=2)
        weight_b = weight.astype(jnp.bfloat16)
        mixed_b = (weight * score_t).astype(jnp.bfloat16)
        factor = shrink.T[:, :, None]
        plain = plain * factor + jnp.einsum(
            "hqk,khd->qhd", weight_b, value_b, preferred_element_type=jnp.float32
        )
        mixed = mixed * factor + jnp.einsum(
            "hqk,khd->qhd", mixed_b, value_b, preferred_element_type=jnp.float32
        )
        carried = carried * factor + jnp.einsum(
            "hqk,khd->qhd", weight_b, value_tb, preferred_element_type=jnp.float32
        )
        return (top_new, total, drift, plain, mixed, carried)

    flat = jnp.zeros((local_heads, rows), jnp.float32)
    wide = jnp.zeros((rows, local_heads, DH), jnp.float32)
    state = (jnp.full((local_heads, rows), -1e30, jnp.float32), flat, flat, wide, wide, wide)
    own = jnp.stack([key, value, key_t, value_t])
    state = update(state, own, earlier_frames[0])
    ahead = own
    for step in range(1, SPAN + 1):
        ahead = passed_along(ahead, "ctx", 1)
        state = update(state, ahead, earlier_frames[step])
    top, total, drift, plain, mixed, carried = state
    total_t = total.T[:, :, None]
    attended = plain / total_t
    attended_tangent = (mixed + carried) / total_t - attended * (drift.T[:, :, None] / total_t)
    return (
        attended.reshape(rows, width).astype(jnp.bfloat16),
        attended_tangent.reshape(rows, width).astype(jnp.bfloat16),
    )


def solution(mesh):
    return jax.shard_map(
        per_device,
        mesh=mesh,
        in_specs=(
            P("ctx", "fsdp"),
            P("ctx", "fsdp"),
            P("ctx"),
            P(),
            P("ctx", "fsdp"),
            P("ctx", "fsdp"),
            P("ctx", "fsdp"),
        ),
        out_specs=(P("ctx", "fsdp"), P("ctx", "fsdp")),
        check_vma=False,
    )
```

profile of v0, /device:TPU:24, one launch (start us, length us, event | category | flops | bytes accessed | tf_op | source)
XLA Modules:
  0.0 461.1 jit_solution(18270169645563129938)
XLA Ops:
  10.6 75.8 %all-gather.6.cloned.1.call-done = bf16[384,5120]{1,0:T(8,128)(2,1)} async-done(((bf16[384,640]{1,0:T(8,128)(2,1)}), bf16[384,5120]{1,0:T(8,128)(2,1)}) %all-gather.6.cloned.1.call-update) | async-done | bytes 3932176 | tf_op jit(solution)/shard_map/all_gather | solution.py:21
  86.3 4.2 constant_dynamic-update-slice_fusion.1
  90.6 70.9 %all-gather.8.cloned.1.call-done = bf16[384,5120]{1,0:T(8,128)(2,1)} async-done(((bf16[384,640]{1,0:T(8,128)(2,1)}), bf16[384,5120]{1,0:T(8,128)(2,1)}) %all-gather.8.cloned.1.call-update) | async-done | bytes 3932176 | tf_op jit(solution)/shard_map/all_gather | solution.py:22
  161.5 4.3 constant_dynamic-update-slice_fusion
  165.8 63.5 %all-gather.12.cloned.1.call-done = bf16[5120,384]{1,0:T(8,128)(2,1)} async-done(((bf16[160,384]{1,0:T(8,128)(2,1)}), bf16[5120,384]{1,0:T(8,128)(2,1)}) %all-gather.12.cloned.1.call-update) | async-done | bytes 3932176 | tf_op jit(solution)/shard_map/all_gather | solution.py:27
  229.2 7.6 %convolution_convert_fusion.1 = bf16[768,384]{0,1:T(8,128)(2,1)S(1)} fusion(bf16[768,5120]{1,0:T(8,128)(2,1)} %constant_dynamic-update-slice_fusion, bf16[5120,384]{1,0:T(8,128)(2,1)} %all-gather.12.cloned.1.call-done), kind=kOutput, calls=%fused_computation.22 | convolution fusion | flops 3020193792 | bytes 12386304 | tf_op jit(solution)/shard_map/dot_general | solution.py:30
  237.1 60.1 %all-gather.14.cloned.1.call-done = bf16[5120,384]{1,0:T(8,128)(2,1)} async-done(((bf16[160,384]{1,0:T(8,128)(2,1)}), bf16[5120,384]{1,0:T(8,128)(2,1)}) %all-gather.14.cloned.1.call-update) | async-done | bytes 3932176 | tf_op jit(solution)/shard_map/all_gather | solution.py:28
  297.3 7.6 %convolution_convert_fusion = bf16[768,384]{0,1:T(8,128)(2,1)S(1)} fusion(bf16[768,5120]{1,0:T(8,128)(2,1)} %constant_dynamic-update-slice_fusion, bf16[5120,384]{1,0:T(8,128)(2,1)} %all-gather.14.cloned.1.call-done), kind=kOutput, calls=%fused_computation.21 | convolution fusion | flops 3020193792 | bytes 12386304 | tf_op jit(solution)/shard_map/dot_general | solution.py:30
  306.1 17.7 %collective-permute-done.1 = bf16[4,384,3,128]{3,1,2,0:T(8,128)(2,1)} collective-permute-done((bf16[4,384,3,128]{3,1,2,0:T(8,128)(2,1)S(1)}, bf16[4,384,3,128]{3,1,2,0:T(8,128)(2,1)}, u32[]{:S(2)}, u32[]{:S(2)}) %collective-permute-start.1) | collective-permute-done | bytes 1179680 | tf_op jit(solution)/shard_map/ppermute | solution.py:13
  323.8 2.5 gather_fusion
  326.9 3.2 collective-permute-start.2
  330.1 2.4 collective-permute-start.4
  332.5 3.9 collective-permute-start.6
  336.4 5.6 %collective-permute-done = s32[384]{0:T(512)S(1)} collective-permute-done((s32[384]{0:T(512)S(1)}, s32[384]{0:T(512)S(1)}, u32[]{:S(2)}, u32[]{:S(2)}) %collective-permute-start) | collective-permute-done | bytes 1568 | tf_op jit(solution)/shard_map/ppermute | solution.py:13
  342.0 6.2 %collective-permute-done.4 = s32[384]{0:T(512)S(1)} collective-permute-done((s32[384]{0:T(512)S(1)}, s32[384]{0:T(512)S(1)}, u32[]{:S(2)}, u32[]{:S(2)}) %collective-permute-start.4) | collective-permute-done | bytes 1568 | tf_op jit(solution)/shard_map/ppermute | solution.py:13
  349.0 46.2 %all-gather.10.cloned.1.call-done = bf16[5120,384]{1,0:T(8,128)(2,1)} async-done(((bf16[160,384]{1,0:T(8,128)(2,1)}), bf16[5120,384]{1,0:T(8,128)(2,1)}) %all-gather.10.cloned.1.call-update) | async-done | bytes 3932176 | tf_op jit(solution)/shard_map/all_gather | solution.py:26
  395.3 7.6 %convolution_convert_fusion.2 = bf16[768,384]{0,1:T(8,128)(2,1)S(1)} fusion(bf16[768,5120]{1,0:T(8,128)(2,1)} %constant_dynamic-update-slice_fusion, bf16[5120,384]{1,0:T(8,128)(2,1)} %all-gather.10.cloned.1.call-done), kind=kOutput, calls=%fused_computation.23 | convolution fusion | flops 3020193792 | bytes 12386304 | tf_op jit(solution)/shard_map/dot_general | solution.py:30
  403.9 1.4 fusion.1
  408.6 1.4 fusion.2
  411.3 1.4 fusion.3
  412.8 10.8 %collective-permute-done.7 = bf16[4,384,3,128]{3,1,2,0:T(8,128)(2,1)S(1)} collective-permute-done((bf16[4,384,3,128]{3,1,2,0:T(8,128)(2,1)}, bf16[4,384,3,128]{3,1,2,0:T(8,128)(2,1)S(1)}, u32[]{:S(2)}, u32[]{:S(2)}) %collective-permute-start.7) | collective-permute-done | bytes 1179680 | tf_op jit(solution)/shard_map/ppermute | solution.py:13
  427.7 1.9 fusion.94
  429.6 1.9 fusion.93
  431.5 1.9 fusion.92
  436.1 1.7 fusion.11
  437.7 1.9 fusion.9
  439.6 1.7 fusion.7
  442.0 1.6 fusion.33
  443.6 1.7 fusion.31
  445.3 1.7 fusion.29
  447.0 1.4 fusion.23
  449.7 1.4 fusion.19
  (60 shorter events, 23.4 us)
Async XLA Ops:
  7.2 316.6 %copy-start = (s32[12288]{0:T(1024)S(1)}, s32[12288]{0:T(1024)}, u32[]{:S(2)}) copy-start(s32[12288]{0:T(1024)} %param.10) | copy-start | bytes 147460
  7.2 79.2 %all-gather.6.cloned.1.call-start = ((), (), s32[]{:S(2)}) async-start(), calls=%async_computation | async-start | bytes 4423680 | tf_op jit(solution)/shard_map/all_gather | solution.py:21
  7.9 153.6 %all-gather.8.cloned.1.call-start = ((), (), s32[]{:S(2)}) async-start(), calls=%async_computation.1 | async-start | bytes 4423680 | tf_op jit(solution)/shard_map/all_gather | solution.py:22
  8.7 220.6 %all-gather.12.cloned.1.call-start = ((), (), s32[]{:S(2)}) async-start(), calls=%async_computation.3 | async-start | bytes 4055040 | tf_op jit(solution)/shard_map/all_gather | solution.py:27
  9.4 287.9 %all-gather.14.cloned.1.call-start = ((), (), s32[]{:S(2)}) async-start(), calls=%async_computation.4 | async-start | bytes 4055040 | tf_op jit(solution)/shard_map/all_gather | solution.py:28
  10.0 385.3 %all-gather.10.cloned.1.call-start = ((), (), s32[]{:S(2)}) async-start(), calls=%async_computation.2 | async-start | bytes 4055040 | tf_op jit(solution)/shard_map/all_gather | solution.py:26
  305.2 18.6 %copy-start.2 = (s32[384]{0:T(512)S(1)}, s32[384]{0:T(512)}, u32[]{:S(2)}) copy-start(s32[384]{0:T(512)} %param.9) | copy-start | bytes 4612
  305.8 18.0 %collective-permute-start.1 = (bf16[4,384,3,128]{3,1,2,0:T(8,128)(2,1)S(1)}, bf16[4,384,3,128]{3,1,2,0:T(8,128)(2,1)}, u32[]{:S(2)}, u32[]{:S(2)}) collective-permute-start(bf16[4,384,3,128]{3,1,2,0:T(8,128)(2,1)S(1)} %pad_maximum_fusion), channel_id=1, source_target_pairs={{248,0},{0,8},{8,16},{16,24},{24,32},{32,40},{40,48},{48,56},{56,6... | collective-permute-start | bytes 3538952 | tf_op jit(solution)/shard_map/ppermute | solution.py:13
  323.8 25.1 %collective-permute-start.3 = (bf16[4,384,3,128]{3,1,2,0:T(8,128)(2,1)}, bf16[4,384,3,128]{3,1,2,0:T(8,128)(2,1)}, u32[]{:S(2)}, u32[]{:S(2)}) collective-permute-start(bf16[4,384,3,128]{3,1,2,0:T(8,128)(2,1)} %collective-permute-done.1), channel_id=1, source_target_pairs={{248,0},{0,8},{8,16},{16,24},{24,32},{32,40},{40,48},{48,56},{56,6... | collective-permute-start | bytes 3538952 | tf_op jit(solution)/shard_map/ppermute | solution.py:13
  326.4 15.6 %collective-permute-start = (s32[384]{0:T(512)S(1)}, s32[384]{0:T(512)S(1)}, u32[]{:S(2)}, u32[]{:S(2)}) collective-permute-start(s32[384]{0:T(512)S(1)} %and_select_fusion), channel_id=1, source_target_pairs={{248,0},{0,8},{8,16},{16,24},{24,32},{32,40},{40,48},{48,56},{56,6... | collective-permute-start | bytes 4616 | tf_op jit(solution)/shard_map/ppermute | solution.py:13
  326.9 15.1 %collective-permute-start.2 = (s32[384]{0:T(512)S(1)}, s32[384]{0:T(512)S(1)}, u32[]{:S(2)}, u32[]{:S(2)}) collective-permute-start(s32[384]{0:T(512)S(1)} %and_select_fusion), channel_id=1, source_target_pairs={{240,0},{248,8},{0,16},{8,24},{16,32},{24,40},{32,48},{40,56},{48,... | collective-permute-start | bytes 4616 | tf_op jit(solution)/shard_map/ppermute | solution.py:13
  330.1 18.2 %collective-permute-start.4 = (s32[384]{0:T(512)S(1)}, s32[384]{0:T(512)S(1)}, u32[]{:S(2)}, u32[]{:S(2)}) collective-permute-start(s32[384]{0:T(512)S(1)} %and_select_fusion), channel_id=1, source_target_pairs={{232,0},{240,8},{248,16},{0,24},{8,32},{16,40},{24,48},{32,56},{40... | collective-permute-start | bytes 4616 | tf_op jit(solution)/shard_map/ppermute | solution.py:13
  332.5 15.7 %collective-permute-start.6 = (s32[384]{0:T(512)S(1)}, s32[384]{0:T(512)S(1)}, u32[]{:S(2)}, u32[]{:S(2)}) collective-permute-start(s32[384]{0:T(512)S(1)} %and_select_fusion), channel_id=1, source_target_pairs={{224,0},{232,8},{240,16},{248,24},{0,32},{8,40},{16,48},{24,56},{3... | collective-permute-start | bytes 4616 | tf_op jit(solution)/shard_map/ppermute | solution.py:13
  348.8 56.5 %collective-permute-start.5 = (bf16[4,384,3,128]{3,1,2,0:T(8,128)(2,1)}, bf16[4,384,3,128]{3,1,2,0:T(8,128)(2,1)}, u32[]{:S(2)}, u32[]{:S(2)}) collective-permute-start(bf16[4,384,3,128]{3,1,2,0:T(8,128)(2,1)} %collective-permute-done.3), channel_id=1, source_target_pairs={{248,0},{0,8},{8,16},{16,24},{24,32},{32,40},{40,48},{48,56},{56,6... | collective-permute-start | bytes 3538952 | tf_op jit(solution)/shard_map/ppermute | solution.py:13
  405.4 18.2 %collective-permute-start.7 = (bf16[4,384,3,128]{3,1,2,0:T(8,128)(2,1)}, bf16[4,384,3,128]{3,1,2,0:T(8,128)(2,1)S(1)}, u32[]{:S(2)}, u32[]{:S(2)}) collective-permute-start(bf16[4,384,3,128]{3,1,2,0:T(8,128)(2,1)} %collective-permute-done.5), channel_id=1, source_target_pairs={{248,0},{0,8},{8,16},{16,24},{24,32},{32,40},{40,48},{48,56},{56,6... | collective-permute-start | bytes 3538952 | tf_op jit(solution)/shard_map/ppermute | solution.py:13
  451.8 2.3 copy-start.1
Sparse Core Ops, SparseCore 0:
  10.6 75.6 all-gather.5
  89.0 72.5 all-gather.7
  163.4 65.8 all-gather.11
  231.0 66.2 all-gather.13
  299.0 96.2 all-gather.9
where the time goes:
time: 470 us; the launch traced here: 461 us
  waiting for transfers between devices  360 us (77%)
  matrix products  58.3 us (12%)
  between operations  14.5 us (3%)
  local copies, waits for them, and re-layouts  13.9 us (3%)
  starting transfers between devices  11.2 us (2%)
    all_gather x1, waiting for transfers between devices, per_device(): lax.all_gather(tokens, 'fsdp', axis=1, tiled=True)  75.8 us
    all_gather x1, waiting for transfers between devices, per_device(): lax.all_gather(tangents, 'fsdp', axis=1, tiled=True)  70.9 us
    all_gather x1, waiting for transfers between devices, per_device(): lax.all_gather(w_key, 'ctx', axis=0, tiled=True)  63.5 us
    all_gather x1, waiting for transfers between devices, per_device(): lax.all_gather(w_value, 'ctx', axis=0, tiled=True)  60.1 us
    all_gather x1, waiting for transfers between devices, per_device(): lax.all_gather(w_query, 'ctx', axis=0, tiled=True)  46.2 us
    ppermute x8, waiting for transfers between devices, passed_along(): return lax.ppermute(block, axis, route)  40.4 us
    dot_general x3, matrix products, per_device(): jnp.dot(stacked, piece, preferred_element_type=jnp.float32)  22.8 us
    ppermute x8, starting transfers between devices, passed_along(): return lax.ppermute(block, axis, route)  11.1 us
  transfers between devices with their start and end apart: 13, of which 9 were waited for; matrix products, arithmetic and copies ran while one was open for 10% of the time, Pallas kernels for 0%

commit v1 on v0

v1 whole, which is shorter than its diff:
```python
import functools

import jax
import jax.numpy as jnp
from jax import lax
from jax.experimental import pallas as pl
from jax.experimental.pallas import tpu as pltpu
from jax.sharding import PartitionSpec as P

MESH = pl.DeviceIdType.MESH
DH = 128
HEADS = 3
SPAN = 4
TOK = 384
FEAT = 640
DEPTH = 160
COLS = HEADS * DH
PARTS = (256, 128)
STARTS = (0, 256)
FRAMES = 8
CTX = 32
SCALE = DH**-0.5
LOG2E = 1.4426950408889634
NT = (((1,), (1,)), ((), ()))
N_REMOTE = 90


def kernel(
    pos_ref, frames_ref, tok_ref, tan_ref, wq_ref, wk_ref, wv_ref,
    att_ref, att_t_ref,
    x0, x1, wkv, wq, kv0, kv1, q_all, fr, qf, acc, top, total, drift, pv, mixed,
    local_sem, send_sem, recv_sem,
):
    xs_all, kvs = (x0, x1), (kv0, kv1)
    i, f = lax.axis_index("ctx"), lax.axis_index("fsdp")
    ylo, z, core = i // 16, (i // 2) % 8, i % 2
    yhi, x = f // 4, f % 4

    def at(yl, zz, cc, yh, xx):
        return (yl * 16 + zz * 2 + cc, yh * 4 + xx)

    right, left = at(ylo, z, core, yhi, (x + 1) % 4), at(ylo, z, core, yhi, (x + 3) % 4)
    across = at(ylo, z, core, 1 - yhi, x)
    beside = at(1 - ylo, z, core, yhi, x)
    up, down = at(ylo, (z + 1) % 8, core, yhi, x), at(ylo, (z + 7) % 8, core, yhi, x)
    sibling = at(ylo, z, 1 - core, yhi, x)
    after = ((i + 2) % CTX, f)

    used = []

    def remote(src, dst, device):
        k = len(used)
        copy = pltpu.make_async_remote_copy(
            src, dst, send_sem.at[k], recv_sem.at[k], device_id=device, device_id_type=MESH
        )
        used.append(copy)
        return copy

    def same(ref, device):
        return remote(ref, ref, device)

    def x_at(part, yh, xx, half=None):
        rows = pl.ds(0, 2 * PARTS[part]) if half is None else pl.ds(half * PARTS[part], PARTS[part])
        return xs_all[part].at[yh * 2 + xx // 2, rows, pl.ds(pl.multiple_of((xx % 2) * FEAT, 128), FEAT)]

    def w_at(ref, yl, zz):
        j = yl * 16 + zz * 2 + core
        return ref.at[j // 8, pl.ds(pl.multiple_of((j % 8) * DEPTH, 32), DEPTH)]

    j_pair, j_row = i // 8, pl.ds(pl.multiple_of((i % 8) * DEPTH, 32), DEPTH)
    loads = [
        pltpu.make_async_copy(wk_ref, wkv.at[j_pair, j_row, pl.ds(0, COLS)], local_sem.at[0]),
        pltpu.make_async_copy(wv_ref, wkv.at[j_pair, j_row, pl.ds(COLS, COLS)], local_sem.at[1]),
        pltpu.make_async_copy(wq_ref, wq.at[j_pair, j_row], local_sem.at[2]),
    ]
    for part in range(2):
        rows = pl.ds(STARTS[part], PARTS[part])
        loads.append(pltpu.make_async_copy(tok_ref.at[rows], x_at(part, yhi, x, 0), local_sem.at[3 + 2 * part]))
        loads.append(pltpu.make_async_copy(tan_ref.at[rows], x_at(part, yhi, x, 1), local_sem.at[4 + 2 * part]))
    for k in (0, 1, 3, 4, 2, 5, 6):
        loads[k].start()

    barrier = pltpu.get_barrier_semaphore()
    greeted = [right, left, across, beside, up, down, sibling]
    for d in range(1, SPAN + 1):
        greeted.append(((i + d) % CTX, f))
        greeted.append(((i + CTX - d) % CTX, f))
    for device in greeted:
        pl.semaphore_signal(barrier, inc=1, device_id=device, device_id_type=MESH)
    pl.semaphore_wait(barrier, len(greeted))

    hops = {("own", 1): 4, ("own", -1): 3, ("other", 1): 3, ("other", -1): 4}
    side = {"own": ylo, "other": 1 - ylo}
    ring, kv_sib = {}, []

    def w_share(which, way, step):
        return w_at(wkv, side[which], (z + 8 - way * step) % 8)

    def w_send(which, way, step):
        ring[which, way, step] = same(w_share(which, way, step), up if way == 1 else down)
        ring[which, way, step].start()

    def w_sib(ref):
        kv_sib.append(same(ref, sibling))
        kv_sib[-1].start()

    def w_turn(which, step):
        for way in (1, -1):
            if step < hops[which, way]:
                ring[which, way, step].wait_recv()
                if step + 1 < hops[which, way]:
                    w_send(which, way, step + 1)
                w_sib(w_share(which, way, step + 1))

    loads[0].wait()
    loads[1].wait()
    swap = same(w_at(wkv, ylo, z), beside)
    swap.start()
    w_send("own", 1, 0)
    w_send("own", -1, 0)

    xc = {}

    def x_send(name, part, ref, device):
        xc[name, part] = same(ref, device)
        xc[name, part].start()

    loads[3].wait()
    loads[4].wait()
    x_send("a", 0, x_at(0, yhi, x), right)
    x_send("b", 0, x_at(0, yhi, x), left)
    x_send("c", 0, x_at(0, yhi, x), across)
    w_sib(w_at(wkv, ylo, z))

    position = pos_ref[...]
    row_frame = jnp.zeros_like(position)
    for number in range(1, FRAMES):
        before = jnp.where(frames_ref[...] < number, 1, 0)
        start = jnp.sum(jnp.sum(before, axis=0, keepdims=True), axis=1, keepdims=True)
        row_frame += jnp.where(position >= start, 1, 0)
    fr[0] = jnp.broadcast_to(row_frame, (8, TOK))
    fr_copies = [remote(fr.at[0], fr.at[d], ((i + d) % CTX, f)) for d in range(1, SPAN + 1)]
    for copy in fr_copies:
        copy.start()
    line = lax.broadcasted_iota(jnp.int32, (TOK, TOK), 0)
    column = lax.broadcasted_iota(jnp.int32, (TOK, TOK), 1)
    turned = jnp.sum(
        jnp.where(line == column, row_frame.astype(jnp.float32), 0.0), axis=1, keepdims=True
    )
    qf[...] = jnp.broadcast_to(turned.astype(jnp.int32), (TOK, 128))

    def x_first(part):
        xc["a", part].wait_recv()
        x_send("d", part, x_at(part, yhi, (x + 3) % 4, 0), right)
        xc["b", part].wait_recv()
        x_send("e", part, x_at(part, yhi, (x + 1) % 4, 1), left)

    def x_second(part):
        xc["c", part].wait_recv()
        x_send("f", part, x_at(part, 1 - yhi, x), right)
        x_send("g", part, x_at(part, 1 - yhi, x), left)

    def x_third(part):
        xc["d", part].wait_recv()
        xc["e", part].wait_recv()
        x_send("h", part, x_at(part, yhi, (x + 2) % 4), across)

    def x_last(part):
        for name in ("f", "g", "h"):
            xc[name, part].wait_recv()

    swap.wait_recv()
    w_send("other", 1, 0)
    w_send("other", -1, 0)
    w_sib(w_at(wkv, 1 - ylo, z))
    w_turn("own", 0)
    x_first(0)
    x_second(0)
    w_turn("other", 0)
    loads[5].wait()
    loads[6].wait()
    x_send("c", 1, x_at(1, yhi, x), across)
    w_turn("own", 1)
    x_third(0)
    x_send("a", 1, x_at(1, yhi, x), right)
    x_send("b", 1, x_at(1, yhi, x), left)
    w_turn("other", 1)
    w_turn("own", 2)
    x_second(1)
    w_turn("other", 2)

    q_ring, q_beside, q_sib = [], [], []

    def q_sibling(ref):
        q_sib.append(same(ref, sibling))
        q_sib[-1].start()

    def q_pass(step):
        share = w_at(wq, ylo, (z + step) % 8)
        if step < 7:
            q_ring.append(same(share, down))
            q_ring[-1].start()
        q_beside.append(same(share, beside))
        q_beside[-1].start()
        q_sibling(share)

    def q_turn(step):
        q_ring[step].wait_recv()
        q_pass(step + 1)
        q_beside[step].wait_recv()
        q_sibling(w_at(wq, 1 - ylo, (z + step) % 8))

    loads[2].wait()
    q_pass(0)
    x_first(1)
    w_turn("own", 3)
    w_turn("other", 3)
    x_third(1)
    x_last(0)
    for copy in kv_sib:
        copy.wait_recv()

    def project(part, weights, width, between):
        rows = 2 * PARTS[part]
        for pair in range(4):
            made = jnp.dot(xs_all[part][pair], weights[pair], preferred_element_type=jnp.float32)
            if pair == 0:
                acc[pl.ds(0, rows), pl.ds(0, width)] = made
            else:
                acc[pl.ds(0, rows), pl.ds(0, width)] += made
            between(pair)

    def keep_kv(part):
        rows = PARTS[part]
        for which in range(2):
            for head in range(HEADS):
                columns = pl.ds(which * COLS + head * DH, DH)
                kvs[part][0, which, :, pl.ds(head * 256, DH)] = acc[pl.ds(0, rows), columns].astype(jnp.bfloat16)
                kvs[part][0, which, :, pl.ds(head * 256 + DH, DH)] = acc[pl.ds(rows, rows), columns].astype(
                    jnp.bfloat16
                )

    kva, kvb, siba, sibb = {}, {}, {}, {}

    def kv_start(part):
        kva[part] = remote(kvs[part].at[0], kvs[part].at[2], after)
        kva[part].start()

    def kv_pass(part):
        kva[part].wait_recv()
        kvb[part] = remote(kvs[part].at[2], kvs[part].at[4], after)
        kvb[part].start()
        siba[part] = remote(kvs[part].at[2 * core], kvs[part].at[1], sibling)
        siba[part].start()

    def kv_end(part):
        kvb[part].wait_recv()
        sibb[part] = remote(kvs[part].at[2 + 2 * core], kvs[part].at[3], sibling)
        sibb[part].start()

    project(0, wkv, 2 * COLS, lambda pair: q_turn(pair) if pair < 3 else None)
    keep_kv(0)
    kv_start(0)
    x_last(1)
    project(1, wkv, 2 * COLS, lambda pair: q_turn(3 + pair) if pair < 2 else None)
    keep_kv(1)
    kv_start(1)
    q_turn(5)
    q_turn(6)
    q_beside[7].wait_recv()
    q_sibling(w_at(wq, 1 - ylo, (z + 7) % 8))
    for copy in q_sib:
        copy.wait_recv()
    kv_pass(0)

    for part in range(2):
        project(part, wq, COLS, lambda pair: None)
        rows, at_row = PARTS[part], STARTS[part]
        for head in range(HEADS):
            columns = pl.ds(head * DH, DH)
            q_all[pl.ds(at_row, rows), pl.ds(head * 256 + DH, DH)] = acc[pl.ds(0, rows), columns].astype(jnp.bfloat16)
            q_all[pl.ds(at_row, rows), pl.ds(head * 256, DH)] = acc[pl.ds(rows, rows), columns].astype(jnp.bfloat16)

    def attend(pieces, first):
        def one_head(head, _):
            wide = pl.ds(pl.multiple_of(head * 256, 256), 256)
            slim = pl.ds(pl.multiple_of(head * 256, 256), DH)
            query = q_all[:, pl.ds(pl.multiple_of(head * 256 + DH, DH), DH)]
            both = q_all[:, wide]
            query_frames = qf[:, 0:1]
            scores, scores_t = [], []
            for slot, part in pieces:
                keys = kvs[part].at[slot, 0]
                score = lax.dot_general(query, keys[:, slim], NT, preferred_element_type=jnp.float32)
                score_t = lax.dot_general(both, keys[:, wide], NT, preferred_element_type=jnp.float32)
                key_frames = fr[slot, 0:1, pl.ds(STARTS[part], PARTS[part])]
                scores.append(jnp.where(key_frames <= query_frames, score * (SCALE * LOG2E), -1e30))
                scores_t.append(score_t)
            here = functools.reduce(jnp.maximum, [jnp.max(s, axis=1, keepdims=True) for s in scores])
            if first:
                top_new = here
            else:
                top_old = top[head, :, 0:1]
                top_new = jnp.maximum(top_old, here)
                shrink = jnp.exp2(top_old - top_new)
            lanes, lanes_t = [], []
            out_v, out_m = None, None
            for (slot, part), score, score_t in zip(pieces, scores, scores_t):
                weight = jnp.exp2(score - top_new)
                moved = weight * score_t
                for c in range(0, PARTS[part], 128):
                    lanes.append(weight[:, c : c + 128])
                    lanes_t.append(moved[:, c : c + 128])
                values = kvs[part].at[slot, 1]
                a = jnp.dot(weight.astype(jnp.bfloat16), values[:, wide], preferred_element_type=jnp.float32)
                b = jnp.dot(moved.astype(jnp.bfloat16), values[:, slim], preferred_element_type=jnp.float32)
                out_v = a if out_v is None else out_v + a
                out_m = b if out_m is None else out_m + b
            add = functools.reduce(jnp.add, lanes)
            add_t = functools.reduce(jnp.add, lanes_t)
            top[head] = jnp.broadcast_to(top_new, (TOK, 128))
            if first:
                total[head], drift[head] = add, add_t
                pv[head], mixed[head] = out_v, out_m
            else:
                total[head] = total[head] * shrink + add
                drift[head] = drift[head] * shrink + add_t
                pv[head] = pv[head] * shrink + out_v
                mixed[head] = mixed[head] * shrink + out_m
            return 0

        lax.fori_loop(0, HEADS, one_head, 0)

    attend([(0, 0), (0, 1)], True)
    for copy in fr_copies:
        copy.wait_recv()
    kv_pass(1)
    siba[0].wait_recv()
    attend([(1, 0), (2, 0)], False)
    siba[1].wait_recv()
    attend([(1, 1), (2, 1)], False)
    kv_end(0)
    sibb[0].wait_recv()
    attend([(3, 0), (4, 0)], False)
    kv_end(1)
    sibb[1].wait_recv()
    attend([(3, 1), (4, 1)], False)

    for head in range(HEADS):
        whole = jnp.sum(total[head], axis=1, keepdims=True)
        pull = jnp.sum(drift[head], axis=1, keepdims=True) * SCALE
        attended = pv[head, :, pl.ds(0, DH)] / whole
        moved = mixed[head] * SCALE + pv[head, :, pl.ds(DH, DH)]
        columns = pl.ds(head * DH, DH)
        att_ref[:, columns] = attended.astype(jnp.bfloat16)
        att_t_ref[:, columns] = (moved / whole - attended * (pull / whole)).astype(jnp.bfloat16)

    for copy in used:
        copy.wait_send()


def per_device(tokens, tangents, positions, frames, w_query, w_key, w_value):
    out = jax.ShapeDtypeStruct((TOK, COLS), jnp.bfloat16)
    vmem = pl.BlockSpec(memory_space=pltpu.VMEM)
    anywhere = pl.BlockSpec(memory_space=pl.ANY)
    bf16, f32 = jnp.bfloat16, jnp.float32
    return pl.pallas_call(
        kernel,
        out_shape=(out, out),
        in_specs=[vmem, vmem] + [anywhere] * 5,
        out_specs=(vmem, vmem),
        scratch_shapes=[
            pltpu.VMEM((4, 2 * PARTS[0], 2 * FEAT), bf16),
            pltpu.VMEM((4, 2 * PARTS[1], 2 * FEAT), bf16),
            pltpu.VMEM((4, 8 * DEPTH, 2 * COLS), bf16),
            pltpu.VMEM((4, 8 * DEPTH, COLS), bf16),
            pltpu.VMEM((SPAN + 1, 2, PARTS[0], 2 * COLS), bf16),
            pltpu.VMEM((SPAN + 1, 2, PARTS[1], 2 * COLS), bf16),
            pltpu.VMEM((TOK, 2 * COLS), bf16),
            pltpu.VMEM((SPAN + 1, 8, TOK), jnp.int32),
            pltpu.VMEM((TOK, 128), jnp.int32),
            pltpu.VMEM((2 * PARTS[0], 2 * COLS), f32),
            pltpu.VMEM((HEADS, TOK, 128), f32),
            pltpu.VMEM((HEADS, TOK, 128), f32),
            pltpu.VMEM((HEADS, TOK, 128), f32),
            pltpu.VMEM((HEADS, TOK, 256), f32),
            pltpu.VMEM((HEADS, TOK, 128), f32),
            pltpu.SemaphoreType.DMA((7,)),
            pltpu.SemaphoreType.DMA((N_REMOTE,)),
            pltpu.SemaphoreType.DMA((N_REMOTE,)),
        ],
        compiler_params=pltpu.CompilerParams(
            collective_id=0, has_side_effects=True, vmem_limit_bytes=56 << 20
        ),
        cost_estimate=pl.CostEstimate(flops=12_500_000_000, bytes_accessed=4_000_000, transcendentals=2_300_000),
        name="fused_attention",
    )(
        positions.reshape(1, TOK), frames.reshape(-1, 128), tokens, tangents, w_query, w_key, w_value
    )


def solution(mesh):
    return jax.shard_map(
        per_device,
        mesh=mesh,
        in_specs=(
            P("ctx", "fsdp"),
            P("ctx", "fsdp"),
            P("ctx"),
            P(),
            P("ctx", "fsdp"),
            P("ctx", "fsdp"),
            P("ctx", "fsdp"),
        ),
        out_specs=(P("ctx", "fsdp"), P("ctx", "fsdp")),
        check_vma=False,
    )
```

time: 470 us -> 163 us (0.35)
  the two profiles are of different devices: /device:TPU:24 before, /device:TPU:1 now
where the time goes in v1:
time: 163 us
  Pallas kernels  159 us (98%)
  local copies, waits for them, and re-layouts  3.71 us (2%)
    pallas_call x1, Pallas kernels, per_device(): pl.pallas_call(kernel, out_shape=(out, out), in_specs=[vmem, vmem] + [any...  159 us

profile of v1, /device:TPU:1, one launch (start us, length us, event | category | flops | bytes accessed | tf_op | source)
XLA Modules:
  0.0 163.3 jit_solution(1114299361872943097)
XLA Ops:
  0.6 1.2 reshape.10.pos_ref
  1.9 159.0 %fused_attention.1 = (bf16[384,384]{1,0:T(8,128)(2,1)}, bf16[384,384]{1,0:T(8,128)(2,1)}) custom-call(s32[1,384]{1,0:T(1,128)} %reshape.10.pos_ref, s32[96,128]{1,0:T(8,128)} %bitcast.1, bf16[384,640]{1,0:T(8,128)(2,1)} %tok_ref.1, bf16[384,640]{1,0:T(8,128)(2,1)} %tan_ref.1, bf16[160,384]{1,0:T(8,128)(2,1)} %wq_ref.1, bf16[160,384]{1,0:T(8,128)(2,1)} %wk_ref.1, ...), custom_call_target="tpu_custom_call" | custom-call | flops 12499999744 | bytes 4000000 | tf_op jit(solution)/shard_map/fused_attention/pallas_call | solution.py:367
  160.8 0.0 copy-start
  160.8 1.7 %copy.11 = bf16[384,384]{1,0:T(8,128)(2,1)} copy(bf16[384,384]{1,0:T(8,128)(2,1)} %get-tuple-element.4) | data formatting | bytes 589824
  162.6 0.0 copy-done
  162.6 0.7 copy.12
Async XLA Ops:
  160.8 1.8 %copy-start = (bf16[384,384]{1,0:T(8,128)(2,1)S(1)}, bf16[384,384]{1,0:T(8,128)(2,1)}, u32[]{:S(2)}) copy-start(bf16[384,384]{1,0:T(8,128)(2,1)} %get-tuple-element.5) | copy-start | bytes 884740

commit v2 on v1

--- a/solution.py
+++ b/solution.py
@@ -15,23 +15,22 @@
 FEAT = 640
 DEPTH = 160
 COLS = HEADS * DH
-PARTS = (256, 128)
-STARTS = (0, 256)
+PART = 128
+PARTS = TOK // PART
 FRAMES = 8
 CTX = 32
 SCALE = DH**-0.5
 LOG2E = 1.4426950408889634
 NT = (((1,), (1,)), ((), ()))
-N_REMOTE = 90
+N_REMOTE = 105
 
 
 def kernel(
     pos_ref, frames_ref, tok_ref, tan_ref, wq_ref, wk_ref, wv_ref,
     att_ref, att_t_ref,
-    x0, x1, wkv, wq, kv0, kv1, q_all, fr, qf, acc, top, total, drift, pv, mixed,
+    xs, wkv, wq, kv, q_all, fr, qf, acc, top, total, drift, pv, mixed,
     local_sem, send_sem, recv_sem,
 ):
-    xs_all, kvs = (x0, x1), (kv0, kv1)
     i, f = lax.axis_index("ctx"), lax.axis_index("fsdp")
     ylo, z, core = i // 16, (i // 2) % 8, i % 2
     yhi, x = f // 4, f % 4
@@ -60,8 +59,8 @@
         return remote(ref, ref, device)
 
     def x_at(part, yh, xx, half=None):
-        rows = pl.ds(0, 2 * PARTS[part]) if half is None else pl.ds(half * PARTS[part], PARTS[part])
-        return xs_all[part].at[yh * 2 + xx // 2, rows, pl.ds(pl.multiple_of((xx % 2) * FEAT, 128), FEAT)]
+        rows = pl.ds(0, 2 * PART) if half is None else pl.ds(half * PART, PART)
+        return xs.at[part, yh * 2 + xx // 2, rows, pl.ds(pl.multiple_of((xx % 2) * FEAT, 128), FEAT)]
 
     def w_at(ref, yl, zz):
         j = yl * 16 + zz * 2 + core
@@ -73,11 +72,11 @@
         pltpu.make_async_copy(wv_ref, wkv.at[j_pair, j_row, pl.ds(COLS, COLS)], local_sem.at[1]),
         pltpu.make_async_copy(wq_ref, wq.at[j_pair, j_row], local_sem.at[2]),
     ]
-    for part in range(2):
-        rows = pl.ds(STARTS[part], PARTS[part])
+    for part in range(PARTS):
+        rows = pl.ds(part * PART, PART)
         loads.append(pltpu.make_async_copy(tok_ref.at[rows], x_at(part, yhi, x, 0), local_sem.at[3 + 2 * part]))
         loads.append(pltpu.make_async_copy(tan_ref.at[rows], x_at(part, yhi, x, 1), local_sem.at[4 + 2 * part]))
-    for k in (0, 1, 3, 4, 2, 5, 6):
+    for k in (0, 1, 3, 4, 2, 5, 6, 7, 8):
         loads[k].start()
 
     barrier = pltpu.get_barrier_semaphore()
@@ -125,11 +124,39 @@
         xc[name, part] = same(ref, device)
         xc[name, part].start()
 
-    loads[3].wait()
-    loads[4].wait()
-    x_send("a", 0, x_at(0, yhi, x), right)
-    x_send("b", 0, x_at(0, yhi, x), left)
-    x_send("c", 0, x_at(0, yhi, x), across)
+    def x_here(part):
+        loads[3 + 2 * part].wait()
+        loads[4 + 2 * part].wait()
+
+    def x_own(part):
+        x_send("a", part, x_at(part, yhi, x), right)
+        x_send("b", part, x_at(part, yhi, x), left)
+
+    def x_swap(part):
+        x_send("c", part, x_at(part, yhi, x), across)
+
+    def x_first(part):
+        xc["a", part].wait_recv()
+        x_send("d", part, x_at(part, yhi, (x + 3) % 4, 0), right)
+        xc["b", part].wait_recv()
+        x_send("e", part, x_at(part, yhi, (x + 1) % 4, 1), left)
+        xc["c", part].wait_recv()
+        x_send("f", part, x_at(part, 1 - yhi, x), right)
+        x_send("g", part, x_at(part, 1 - yhi, x), left)
+
+    def x_second(part):
+        xc["f", part].wait_recv()
+        x_send("h", part, x_at(part, 1 - yhi, (x + 3) % 4, 0), right)
+        xc["g", part].wait_recv()
+        x_send("i", part, x_at(part, 1 - yhi, (x + 1) % 4, 1), left)
+
+    def x_last(part):
+        for name in ("d", "e", "h", "i"):
+            xc[name, part].wait_recv()
+
+    x_here(0)
+    x_own(0)
+    x_swap(0)
     w_sib(w_at(wkv, ylo, z))
 
     position = pos_ref[...]
@@ -149,137 +176,129 @@
     )
     qf[...] = jnp.broadcast_to(turned.astype(jnp.int32), (TOK, 128))
 
-    def x_first(part):
-        xc["a", part].wait_recv()
-        x_send("d", part, x_at(part, yhi, (x + 3) % 4, 0), right)
-        xc["b", part].wait_recv()
-        x_send("e", part, x_at(part, yhi, (x + 1) % 4, 1), left)
-
-    def x_second(part):
-        xc["c", part].wait_recv()
-        x_send("f", part, x_at(part, 1 - yhi, x), right)
-        x_send("g", part, x_at(part, 1 - yhi, x), left)
-
-    def x_third(part):
-        xc["d", part].wait_recv()
-        xc["e", part].wait_recv()
-        x_send("h", part, x_at(part, yhi, (x + 2) % 4), across)
-
-    def x_last(part):
-        for name in ("f", "g", "h"):
-            xc[name, part].wait_recv()
+    q_ring, q_sib = {}, []
+
+    def q_sibling(ref):
+        q_sib.append(same(ref, sibling))
+        q_sib[-1].start()
+
+    def q_pass(which, step):
+        share = w_at(wq, side[which], (z + step) % 8)
+        if step < 7:
+            q_ring[which, step] = same(share, down)
+            q_ring[which, step].start()
+        q_sibling(share)
+
+    def q_turn(step):
+        for which in ("own", "other"):
+            q_ring[which, step].wait_recv()
+            q_pass(which, step + 1)
 
     swap.wait_recv()
     w_send("other", 1, 0)
     w_send("other", -1, 0)
     w_sib(w_at(wkv, 1 - ylo, z))
+    for part in range(1, PARTS):
+        x_here(part)
+        x_swap(part)
     w_turn("own", 0)
     x_first(0)
+    loads[2].wait()
+    q_swap = same(w_at(wq, ylo, z), beside)
+    q_swap.start()
+    w_turn("other", 0)
+    w_turn("own", 1)
     x_second(0)
-    w_turn("other", 0)
-    loads[5].wait()
-    loads[6].wait()
-    x_send("c", 1, x_at(1, yhi, x), across)
-    w_turn("own", 1)
-    x_third(0)
-    x_send("a", 1, x_at(1, yhi, x), right)
-    x_send("b", 1, x_at(1, yhi, x), left)
+    x_own(1)
     w_turn("other", 1)
     w_turn("own", 2)
-    x_second(1)
+    x_first(1)
     w_turn("other", 2)
-
-    q_ring, q_beside, q_sib = [], [], []
-
-    def q_sibling(ref):
-        q_sib.append(same(ref, sibling))
-        q_sib[-1].start()
-
-    def q_pass(step):
-        share = w_at(wq, ylo, (z + step) % 8)
-        if step < 7:
-            q_ring.append(same(share, down))
-            q_ring[-1].start()
-        q_beside.append(same(share, beside))
-        q_beside[-1].start()
-        q_sibling(share)
-
-    def q_turn(step):
-        q_ring[step].wait_recv()
-        q_pass(step + 1)
-        q_beside[step].wait_recv()
-        q_sibling(w_at(wq, 1 - ylo, (z + step) % 8))
-
-    loads[2].wait()
-    q_pass(0)
-    x_first(1)
+    q_swap.wait_recv()
+    q_pass("own", 0)
+    q_pass("other", 0)
     w_turn("own", 3)
     w_turn("other", 3)
-    x_third(1)
     x_last(0)
     for copy in kv_sib:
         copy.wait_recv()
 
-    def project(part, weights, width, between):
-        rows = 2 * PARTS[part]
+    def project(part, weights, width):
         for pair in range(4):
-            made = jnp.dot(xs_all[part][pair], weights[pair], preferred_element_type=jnp.float32)
+            made = jnp.dot(xs[part, pair], weights[pair], preferred_element_type=jnp.float32)
             if pair == 0:
-                acc[pl.ds(0, rows), pl.ds(0, width)] = made
+                acc[:, pl.ds(0, width)] = made
             else:
-                acc[pl.ds(0, rows), pl.ds(0, width)] += made
-            between(pair)
+                acc[:, pl.ds(0, width)] += made
+
+    def rows_of(part):
+        return pl.ds(part * PART, PART)
 
     def keep_kv(part):
-        rows = PARTS[part]
         for which in range(2):
             for head in range(HEADS):
                 columns = pl.ds(which * COLS + head * DH, DH)
-                kvs[part][0, which, :, pl.ds(head * 256, DH)] = acc[pl.ds(0, rows), columns].astype(jnp.bfloat16)
-                kvs[part][0, which, :, pl.ds(head * 256 + DH, DH)] = acc[pl.ds(rows, rows), columns].astype(
+                kv[0, which, rows_of(part), pl.ds(head * 256, DH)] = acc[pl.ds(0, PART), columns].astype(jnp.bfloat16)
+                kv[0, which, rows_of(part), pl.ds(head * 256 + DH, DH)] = acc[pl.ds(PART, PART), columns].astype(
                     jnp.bfloat16
                 )
 
     kva, kvb, siba, sibb = {}, {}, {}, {}
 
+    def kv_at(slot, part):
+        return kv.at[slot, :, rows_of(part)]
+
     def kv_start(part):
-        kva[part] = remote(kvs[part].at[0], kvs[part].at[2], after)
+        kva[part] = remote(kv_at(0, part), kv_at(2, part), after)
         kva[part].start()
 
     def kv_pass(part):
         kva[part].wait_recv()
-        kvb[part] = remote(kvs[part].at[2], kvs[part].at[4], after)
+        kvb[part] = remote(kv_at(2, part), kv_at(4, part), after)
         kvb[part].start()
-        siba[part] = remote(kvs[part].at[2 * core], kvs[part].at[1], sibling)
+        siba[part] = remote(kv_at(2 * core, part), kv_at(1, part), sibling)
         siba[part].start()
 
     def kv_end(part):
         kvb[part].wait_recv()
-        sibb[part] = remote(kvs[part].at[2 + 2 * core], kvs[part].at[3], sibling)
+        sibb[part] = remote(kv_at(2 + 2 * core, part), kv_at(3, part), sibling)
         sibb[part].start()
 
-    project(0, wkv, 2 * COLS, lambda pair: q_turn(pair) if pair < 3 else None)
+    project(0, wkv, 2 * COLS)
     keep_kv(0)
     kv_start(0)
+    x_second(1)
+    x_own(2)
+    q_turn(0)
+    q_turn(1)
     x_last(1)
-    project(1, wkv, 2 * COLS, lambda pair: q_turn(3 + pair) if pair < 2 else None)
+    project(1, wkv, 2 * COLS)
     keep_kv(1)
     kv_start(1)
+    kv_pass(0)
+    x_first(2)
+    q_turn(2)
+    kv_pass(1)
+    q_turn(3)
+    x_second(2)
+    q_turn(4)
+    x_last(2)
+    project(2, wkv, 2 * COLS)
+    keep_kv(2)
+    kv_start(2)
     q_turn(5)
+    kv_end(0)
     q_turn(6)
-    q_beside[7].wait_recv()
-    q_sibling(w_at(wq, 1 - ylo, (z + 7) % 8))
     for copy in q_sib:
         copy.wait_recv()
-    kv_pass(0)
-
-    for part in range(2):
-        project(part, wq, COLS, lambda pair: None)
-        rows, at_row = PARTS[part], STARTS[part]
+    kv_end(1)
+
+    for part in range(PARTS):
+        project(part, wq, COLS)
         for head in range(HEADS):
             columns = pl.ds(head * DH, DH)
-            q_all[pl.ds(at_row, rows), pl.ds(head * 256 + DH, DH)] = acc[pl.ds(0, rows), columns].astype(jnp.bfloat16)
-            q_all[pl.ds(at_row, rows), pl.ds(head * 256, DH)] = acc[pl.ds(rows, rows), columns].astype(jnp.bfloat16)
+            q_all[rows_of(part), pl.ds(head * 256 + DH, DH)] = acc[pl.ds(0, PART), columns].astype(jnp.bfloat16)
+            q_all[rows_of(part), pl.ds(head * 256, DH)] = acc[pl.ds(PART, PART), columns].astype(jnp.bfloat16)
 
     def attend(pieces, first):
         def one_head(head, _):
@@ -289,11 +308,11 @@
             both = q_all[:, wide]
             query_frames = qf[:, 0:1]
             scores, scores_t = [], []
-            for slot, part in pieces:
-                keys = kvs[part].at[slot, 0]
+            for slot, start, size in pieces:
+                keys = kv.at[slot, 0, pl.ds(start, size)]
                 score = lax.dot_general(query, keys[:, slim], NT, preferred_element_type=jnp.float32)
                 score_t = lax.dot_general(both, keys[:, wide], NT, preferred_element_type=jnp.float32)
-                key_frames = fr[slot, 0:1, pl.ds(STARTS[part], PARTS[part])]
+                key_frames = fr[slot, 0:1, pl.ds(start, size)]
                 scores.append(jnp.where(key_frames <= query_frames, score * (SCALE * LOG2E), -1e30))
                 scores_t.append(score_t)
             here = functools.reduce(jnp.maximum, [jnp.max(s, axis=1, keepdims=True) for s in scores])
@@ -305,13 +324,13 @@
                 shrink = jnp.exp2(top_old - top_new)
             lanes, lanes_t = [], []
             out_v, out_m = None, None
-            for (slot, part), score, score_t in zip(pieces, scores, scores_t):
+            for (slot, start, size), score, score_t in zip(pieces, scores, scores_t):
                 weight = jnp.exp2(score - top_new)
                 moved = weight * score_t
-                for c in range(0, PARTS[part], 128):
+                for c in range(0, size, 128):
                     lanes.append(weight[:, c : c + 128])
                     lanes_t.append(moved[:, c : c + 128])
-                values = kvs[part].at[slot, 1]
+                values = kv.at[slot, 1, pl.ds(start, size)]
                 a = jnp.dot(weight.astype(jnp.bfloat16), values[:, wide], preferred_element_type=jnp.float32)
                 b = jnp.dot(moved.astype(jnp.bfloat16), values[:, slim], preferred_element_type=jnp.float32)
                 out_v = a if out_v is None else out_v + a
@@ -331,20 +350,22 @@
 
         lax.fori_loop(0, HEADS, one_head, 0)
 
-    attend([(0, 0), (0, 1)], True)
+    early = 2 * PART
+    attend([(0, 0, TOK)], True)
+    kv_pass(2)
     for copy in fr_copies:
         copy.wait_recv()
-    kv_pass(1)
-    siba[0].wait_recv()
-    attend([(1, 0), (2, 0)], False)
-    siba[1].wait_recv()
-    attend([(1, 1), (2, 1)], False)
-    kv_end(0)
-    sibb[0].wait_recv()
-    attend([(3, 0), (4, 0)], False)
-    kv_end(1)
-    sibb[1].wait_recv()
-    attend([(3, 1), (4, 1)], False)
+    for part in range(2):
+        siba[part].wait_recv()
+    attend([(1, 0, early), (2, 0, early)], False)
+    for part in range(2):
+        sibb[part].wait_recv()
+    attend([(3, 0, early), (4, 0, early)], False)
+    siba[2].wait_recv()
+    attend([(1, early, PART), (2, early, PART)], False)
+    kv_end(2)
+    sibb[2].wait_recv()
+    attend([(3, early, PART), (4, early, PART)], False)
 
     for head in range(HEADS):
         whole = jnp.sum(total[head], axis=1, keepdims=True)
@@ -355,6 +376,7 @@
         att_ref[:, columns] = attended.astype(jnp.bfloat16)
         att_t_ref[:, columns] = (moved / whole - attended * (pull / whole)).astype(jnp.bfloat16)
 
+    assert len(used) == N_REMOTE
     for copy in used:
         copy.wait_send()
 
@@ -370,22 +392,20 @@
         in_specs=[vmem, vmem] + [anywhere] * 5,
         out_specs=(vmem, vmem),
         scratch_shapes=[
-            pltpu.VMEM((4, 2 * PARTS[0], 2 * FEAT), bf16),
-            pltpu.VMEM((4, 2 * PARTS[1], 2 * FEAT), bf16),
+            pltpu.VMEM((PARTS, 4, 2 * PART, 2 * FEAT), bf16),
             pltpu.VMEM((4, 8 * DEPTH, 2 * COLS), bf16),
             pltpu.VMEM((4, 8 * DEPTH, COLS), bf16),
-            pltpu.VMEM((SPAN + 1, 2, PARTS[0], 2 * COLS), bf16),
-            pltpu.VMEM((SPAN + 1, 2, PARTS[1], 2 * COLS), bf16),
+            pltpu.VMEM((SPAN + 1, 2, TOK, 2 * COLS), bf16),
             pltpu.VMEM((TOK, 2 * COLS), bf16),
             pltpu.VMEM((SPAN + 1, 8, TOK), jnp.int32),
             pltpu.VMEM((TOK, 128), jnp.int32),
-            pltpu.VMEM((2 * PARTS[0], 2 * COLS), f32),
+            pltpu.VMEM((2 * PART, 2 * COLS), f32),
             pltpu.VMEM((HEADS, TOK, 128), f32),
             pltpu.VMEM((HEADS, TOK, 128), f32),
             pltpu.VMEM((HEADS, TOK, 128), f32),
             pltpu.VMEM((HEADS, TOK, 256), f32),
             pltpu.VMEM((HEADS, TOK, 128), f32),
-            pltpu.SemaphoreType.DMA((7,)),
+            pltpu.SemaphoreType.DMA((3 + 2 * PARTS,)),
             pltpu.SemaphoreType.DMA((N_REMOTE,)),
             pltpu.SemaphoreType.DMA((N_REMOTE,)),
         ],

time: 163 us -> 130 us (0.80)
  Pallas kernels: 159 us -> 125 us
    pallas_call x1, Pallas kernels: 159 us -> 125 us  [per_device(): pl.pallas_call(kernel, out_shape=(out, out), in_specs=[vmem, vmem] + [any...]
where the time goes in v2:
time: 130 us; the launch traced here: 129 us
  Pallas kernels  125 us (96%)
  local copies, waits for them, and re-layouts  3.71 us (3%)
    pallas_call x1, Pallas kernels, per_device(): pl.pallas_call(kernel, out_shape=(out, out), in_specs=[vmem, vmem] + [any...  125 us

profile of v2, /device:TPU:1, one launch (start us, length us, event | category | flops | bytes accessed | tf_op | source)
XLA Modules:
  0.0 129.5 jit_solution(4036900055319410342)
XLA Ops:
  0.6 1.2 reshape.10.pos_ref
  1.9 125.1 %fused_attention.1 = (bf16[384,384]{1,0:T(8,128)(2,1)}, bf16[384,384]{1,0:T(8,128)(2,1)}) custom-call(s32[1,384]{1,0:T(1,128)} %reshape.10.pos_ref, s32[96,128]{1,0:T(8,128)} %bitcast.1, bf16[384,640]{1,0:T(8,128)(2,1)} %tok_ref.1, bf16[384,640]{1,0:T(8,128)(2,1)} %tan_ref.1, bf16[160,384]{1,0:T(8,128)(2,1)} %wq_ref.1, bf16[160,384]{1,0:T(8,128)(2,1)} %wk_ref.1, ...), custom_call_target="tpu_custom_call" | custom-call | flops 12499999744 | bytes 4000000 | tf_op jit(solution)/shard_map/fused_attention/pallas_call | solution.py:389
  127.0 0.0 copy-start
  127.0 1.7 %copy.11 = bf16[384,384]{1,0:T(8,128)(2,1)} copy(bf16[384,384]{1,0:T(8,128)(2,1)} %get-tuple-element.4) | data formatting | bytes 589824
  128.7 0.0 copy-done
  128.7 0.7 copy.12
Async XLA Ops:
  127.0 1.8 %copy-start = (bf16[384,384]{1,0:T(8,128)(2,1)S(1)}, bf16[384,384]{1,0:T(8,128)(2,1)}, u32[]{:S(2)}) copy-start(bf16[384,384]{1,0:T(8,128)(2,1)} %get-tuple-element.5) | copy-start | bytes 884740

commit v3 on v2

v3 whole, which is shorter than its diff:
```python
import functools

import jax
import jax.numpy as jnp
from jax import lax
from jax.experimental import pallas as pl
from jax.experimental.pallas import tpu as pltpu
from jax.sharding import PartitionSpec as P

MESH = pl.DeviceIdType.MESH
DH = 128
HEADS = 3
SPAN = 4
TOK = 384
FEAT = 640
DEPTH = 160
COLS = HEADS * DH
PART = 128
PARTS = TOK // PART
FRAMES = 8
CTX = 32
SCALE = DH**-0.5
LOG2E = 1.4426950408889634
NT = (((1,), (1,)), ((), ()))
N_REMOTE = 164


def kernel(
    pos_ref, frames_ref, tok_ref, tan_ref, wq_ref, wk_ref, wv_ref,
    att_ref, att_t_ref,
    xs, wkv, wq, kv, q_all, fr, qf, acc, top, total, drift, pv, mixed,
    local_sem, send_sem, recv_sem,
):
    i, f = lax.axis_index("ctx"), lax.axis_index("fsdp")
    ylo, z, core = i // 16, (i // 2) % 8, i % 2
    yhi, x = f // 4, f % 4

    def at(yl, zz, cc, yh, xx):
        return (yl * 16 + zz * 2 + cc, yh * 4 + xx)

    right, left = at(ylo, z, core, yhi, (x + 1) % 4), at(ylo, z, core, yhi, (x + 3) % 4)
    across = at(ylo, z, core, 1 - yhi, x)
    beside = at(1 - ylo, z, core, yhi, x)
    up, down = at(ylo, (z + 1) % 8, core, yhi, x), at(ylo, (z + 7) % 8, core, yhi, x)
    sibling = at(ylo, z, 1 - core, yhi, x)
    after = ((i + 2) % CTX, f)

    used = []

    def remote(src, dst, device):
        k = len(used)
        copy = pltpu.make_async_remote_copy(
            src, dst, send_sem.at[k], recv_sem.at[k], device_id=device, device_id_type=MESH
        )
        used.append(copy)
        return copy

    def same(ref, device):
        return remote(ref, ref, device)

    def x_at(part, yh, xx, half=None):
        rows = pl.ds(0, 2 * PART) if half is None else pl.ds(half * PART, PART)
        return xs.at[part, yh * 2 + xx // 2, rows, pl.ds(pl.multiple_of((xx % 2) * FEAT, 128), FEAT)]

    def w_at(yl, zz, columns=slice(None)):
        j = yl * 16 + zz * 2 + core
        return wkv.at[j // 8, pl.ds(pl.multiple_of((j % 8) * DEPTH, 32), DEPTH), columns]

    j_pair, j_row = i // 8, pl.ds(pl.multiple_of((i % 8) * DEPTH, 32), DEPTH)
    loads = [
        pltpu.make_async_copy(wk_ref, wkv.at[j_pair, j_row, pl.ds(0, COLS)], local_sem.at[0]),
        pltpu.make_async_copy(wv_ref, wkv.at[j_pair, j_row, pl.ds(COLS, COLS)], local_sem.at[1]),
    ]
    for head in range(HEADS):
        loads.append(
            pltpu.make_async_copy(wq_ref.at[:, pl.ds(head * DH, DH)], wq.at[head, i // 2, core], local_sem.at[2 + head])
        )
    for part in range(PARTS):
        rows = pl.ds(part * PART, PART)
        loads.append(pltpu.make_async_copy(tok_ref.at[rows], x_at(part, yhi, x, 0), local_sem.at[5 + 2 * part]))
        loads.append(pltpu.make_async_copy(tan_ref.at[rows], x_at(part, yhi, x, 1), local_sem.at[6 + 2 * part]))
    for k in (0, 1, 5, 6, 2, 3, 4, 7, 8, 9, 10):
        loads[k].start()

    barrier = pltpu.get_barrier_semaphore()
    greeted = [right, left, across, beside, up, down, sibling, after, ((i + CTX - 2) % CTX, f)]
    for device in greeted:
        pl.semaphore_signal(barrier, inc=1, device_id=device, device_id_type=MESH)
    pl.semaphore_wait(barrier, len(greeted))

    hops = {
        ("key", "own", 1): 4, ("key", "own", -1): 3, ("key", "other", 1): 3, ("key", "other", -1): 3,
        ("value", "own", 1): 3, ("value", "own", -1): 4, ("value", "other", 1): 3, ("value", "other", -1): 3,
    }
    side = {"own": ylo, "other": 1 - ylo}
    spans = {"key": pl.ds(0, COLS), "value": pl.ds(COLS, COLS)}
    ring, swap, kv_sib, sent = {}, {}, [], []

    def w_share(kind, which, way, step):
        return w_at(side[which], (z + 8 - way * step) % 8, spans[kind])

    def w_send(kind, which, step):
        for way in (1, -1):
            if step < hops[kind, which, way]:
                ring[kind, which, way, step] = same(w_share(kind, which, way, step), up if way == 1 else down)
                ring[kind, which, way, step].start()

    def w_sib(ref):
        kv_sib.append(same(ref, sibling))
        kv_sib[-1].start()

    def w_turn(kind, which, step):
        for way in (1, -1):
            if step < hops[kind, which, way]:
                ring[kind, which, way, step].wait_recv()
        w_send(kind, which, step + 1)
        for way in (1, -1):
            if step < hops[kind, which, way]:
                w_sib(w_share(kind, which, way, step + 1))

    def w_swap(kind):
        swap[kind] = same(w_at(ylo, z, spans[kind]), beside)
        swap[kind].start()
        w_send(kind, "own", 0)

    def w_far(kind):
        swap[kind, 4] = same(w_at(ylo, (z + 4) % 8, spans[kind]), beside)
        swap[kind, 4].start()

    def w_far_end(kind):
        swap[kind, 4].wait_recv()
        w_sib(w_at(1 - ylo, (z + 4) % 8, spans[kind]))

    def w_swapped(kind):
        swap[kind].wait_recv()
        w_send(kind, "other", 0)
        w_sib(w_at(1 - ylo, z, spans[kind]))

    loads[0].wait()
    loads[1].wait()
    w_swap("key")

    xc = {}

    def x_send(name, part, ref, device):
        xc[name, part] = same(ref, device)
        xc[name, part].start()

    def x_here(part):
        loads[5 + 2 * part].wait()
        loads[6 + 2 * part].wait()

    def x_own(part):
        x_send("a", part, x_at(part, yhi, x), right)
        x_send("b", part, x_at(part, yhi, x), left)

    def x_swap(part):
        x_send("c", part, x_at(part, yhi, x), across)

    def x_first(part):
        xc["a", part].wait_recv()
        x_send("d", part, x_at(part, yhi, (x + 3) % 4, 0), right)
        xc["b", part].wait_recv()
        x_send("e", part, x_at(part, yhi, (x + 1) % 4, 1), left)
        xc["c", part].wait_recv()
        x_send("f", part, x_at(part, 1 - yhi, x), right)
        x_send("g", part, x_at(part, 1 - yhi, x), left)

    def x_second(part):
        xc["f", part].wait_recv()
        x_send("h", part, x_at(part, 1 - yhi, (x + 3) % 4, 0), right)
        xc["g", part].wait_recv()
        x_send("i", part, x_at(part, 1 - yhi, (x + 1) % 4, 1), left)

    def x_last(part):
        for name in ("d", "e", "h", "i"):
            xc[name, part].wait_recv()

    x_here(0)
    x_own(0)
    x_swap(0)
    w_sib(w_at(ylo, z))

    position = pos_ref[...].reshape(1, TOK)
    row_frame = jnp.zeros_like(position)
    for number in range(1, FRAMES):
        before = jnp.where(frames_ref[...] < number, 1, 0)
        start = jnp.sum(jnp.sum(before, axis=0, keepdims=True), axis=1, keepdims=True)
        row_frame += jnp.where(position >= start, 1, 0)
    fr[0] = jnp.broadcast_to(row_frame, (8, TOK))
    fr_copies = [remote(fr.at[0], fr.at[2], after)]
    fr_copies[0].start()

    def fr_pass():
        fr_copies[0].wait_recv()
        fr_copies.append(remote(fr.at[2], fr.at[4], after))
        fr_copies.append(remote(fr.at[2 * core], fr.at[1], sibling))
        fr_copies[1].start()
        fr_copies[2].start()

    def fr_end():
        fr_copies[1].wait_recv()
        fr_copies.append(remote(fr.at[2 + 2 * core], fr.at[3], sibling))
        fr_copies[3].start()
    line = lax.broadcasted_iota(jnp.int32, (TOK, TOK), 0)
    column = lax.broadcasted_iota(jnp.int32, (TOK, TOK), 1)
    turned = jnp.sum(
        jnp.where(line == column, row_frame.astype(jnp.float32), 0.0), axis=1, keepdims=True
    )
    qf[...] = jnp.broadcast_to(turned.astype(jnp.int32), (TOK, 128))

    q_ring, q_swap, q_sib = {}, {}, {}

    def q_share(head, which, step):
        return wq.at[head, side[which] * 8 + (z + step) % 8, core]

    def q_up(head):
        for which in ("own", "other"):
            q_ring[head, which, -1] = same(q_share(head, which, 0), up)
            q_ring[head, which, -1].start()

    def q_pass(head, step):
        for which in ("own", "other"):
            q_ring[head, which, step] = same(q_share(head, which, step), down)
            q_ring[head, which, step].start()

    def q_turn(head, step):
        for which in ("own", "other"):
            q_ring[head, which, step].wait_recv()
        if step < 5:
            q_pass(head, step + 1)
        else:
            for which in ("own", "other"):
                q_ring[head, which, -1].wait_recv()
            q_sib[head] = same(wq.at[head, :, core], sibling)
            q_sib[head].start()

    ring["key", "own", 1, 0].wait_send()
    sent.append(ring["key", "own", 1, 0])
    w_swap("value")
    w_turn("key", "own", 0)
    w_swapped("key")
    w_turn("value", "own", 0)
    w_swapped("value")
    x_here(1)
    x_swap(1)
    x_first(0)
    for head in range(HEADS):
        loads[2 + head].wait()
        q_swap[head] = same(q_share(head, "own", 0), beside)
        q_swap[head].start()
    w_turn("key", "own", 1)
    w_turn("key", "other", 0)
    w_turn("value", "own", 1)
    x_here(2)
    x_swap(2)
    w_turn("value", "other", 0)
    fr_pass()
    x_second(0)
    x_own(1)
    w_turn("key", "own", 2)
    w_turn("key", "other", 1)
    w_turn("value", "own", 2)
    w_turn("value", "other", 1)
    x_first(1)
    w_turn("key", "own", 3)
    w_far("key")
    w_turn("value", "own", 3)
    w_far("value")
    for head in range(HEADS):
        q_swap[head].wait_recv()
        q_up(head)
    q_pass(0, 0)
    w_turn("key", "other", 2)
    q_pass(1, 0)
    w_turn("value", "other", 2)
    fr_end()
    x_last(0)

    def project(part, pairs=range(4), first=True):
        for pair in pairs:
            made = jnp.dot(xs[part, pair], wkv[pair], preferred_element_type=jnp.float32)
            if first:
                acc[...] = made
            else:
                acc[...] += made
            first = False

    def rows_of(part):
        return pl.ds(part * PART, PART)

    kva, kvb, siba, sibb = {}, {}, {}, {}

    def kv_at(slot, which, part):
        return kv.at[slot, which, rows_of(part)]

    def kv_start(part):
        for which in range(2):
            for head in range(HEADS):
                columns = pl.ds(which * COLS + head * DH, DH)
                kv[0, which, rows_of(part), pl.ds(head * 256, DH)] = acc[pl.ds(0, PART), columns].astype(jnp.bfloat16)
                kv[0, which, rows_of(part), pl.ds(head * 256 + DH, DH)] = acc[pl.ds(PART, PART), columns].astype(
                    jnp.bfloat16
                )
            kva[which, part] = remote(kv_at(0, which, part), kv_at(2, which, part), after)
            kva[which, part].start()

    def kv_pass(part):
        for which in range(2):
            kva[which, part].wait_recv()
            kvb[which, part] = remote(kv_at(2, which, part), kv_at(4, which, part), after)
            kvb[which, part].start()
        for which in range(2):
            siba[which, part] = remote(kv_at(2 * core, which, part), kv_at(1, which, part), sibling)
            siba[which, part].start()

    def kv_end(part):
        for which in range(2):
            kvb[which, part].wait_recv()
            sibb[which, part] = remote(kv_at(2 + 2 * core, which, part), kv_at(3, which, part), sibling)
            sibb[which, part].start()

    def arrived(copies, part):
        for which in range(2):
            copies[which, part].wait_recv()

    def ask(head, parts=range(PARTS)):
        for part in parts:
            made = jnp.zeros((2 * PART, DH), jnp.float32)
            for pair in range(4):
                weights = wq[head, pl.ds(pair * 4, 4)].reshape(8 * DEPTH, DH)
                made += jnp.dot(xs[part, pair], weights, preferred_element_type=jnp.float32)
            q_all[rows_of(part), pl.ds(head * 256 + DH, DH)] = made[:PART].astype(jnp.bfloat16)
            q_all[rows_of(part), pl.ds(head * 256, DH)] = made[PART:].astype(jnp.bfloat16)

    def attend(heads, pieces, first=False, last=False):
        def one_head(head, _):
            wide = pl.ds(pl.multiple_of(head * 256, 256), 256)
            slim = pl.ds(pl.multiple_of(head * 256, 256), DH)
            query = q_all[:, pl.ds(pl.multiple_of(head * 256 + DH, DH), DH)]
            both = q_all[:, wide]
            slim_out = pl.ds(pl.multiple_of(head * DH, DH), DH)
            query_frames = qf[:, 0:1]
            scores, scores_t = [], []
            for slot, start, size in pieces:
                keys = kv.at[slot, 0, pl.ds(start, size)]
                score = lax.dot_general(query, keys[:, slim], NT, preferred_element_type=jnp.float32)
                score_t = lax.dot_general(both, keys[:, wide], NT, preferred_element_type=jnp.float32)
                key_frames = fr[slot, 0:1, pl.ds(start, size)]
                scores.append(jnp.where(key_frames <= query_frames, score * (SCALE * LOG2E), -1e30))
                scores_t.append(score_t)
            here = functools.reduce(jnp.maximum, [jnp.max(s, axis=1, keepdims=True) for s in scores])
            if first:
                top_new = here
            else:
                top_old = top[head, :, 0:1]
                top_new = jnp.maximum(top_old, here)
                shrink = jnp.exp2(top_old - top_new)
            lanes, lanes_t = [], []
            out_v, out_m = None, None
            for (slot, start, size), score, score_t in zip(pieces, scores, scores_t):
                weight = jnp.exp2(score - top_new)
                moved = weight * score_t
                for c in range(0, size, 128):
                    lanes.append(weight[:, c : c + 128])
                    lanes_t.append(moved[:, c : c + 128])
                values = kv.at[slot, 1, pl.ds(start, size)]
                a = jnp.dot(weight.astype(jnp.bfloat16), values[:, wide], preferred_element_type=jnp.float32)
                b = jnp.dot(moved.astype(jnp.bfloat16), values[:, slim], preferred_element_type=jnp.float32)
                out_v = a if out_v is None else out_v + a
                out_m = b if out_m is None else out_m + b
            add = functools.reduce(jnp.add, lanes)
            add_t = functools.reduce(jnp.add, lanes_t)
            if last:
                whole = jnp.sum(total[head] * shrink + add, axis=1, keepdims=True)
                pull = jnp.sum(drift[head] * shrink + add_t, axis=1, keepdims=True) * SCALE
                out_v += pv[head] * shrink
                out_m += mixed[head] * shrink
                attended = out_v[:, :DH] / whole
                moved = out_m * SCALE + out_v[:, DH:]
                att_ref[:, slim_out] = attended.astype(jnp.bfloat16)
                att_t_ref[:, slim_out] = (moved / whole - attended * (pull / whole)).astype(jnp.bfloat16)
                return 0
            top[head] = jnp.broadcast_to(top_new, (TOK, 128))
            if first:
                total[head], drift[head] = add, add_t
                pv[head], mixed[head] = out_v, out_m
            else:
                total[head] = total[head] * shrink + add
                drift[head] = drift[head] * shrink + add_t
                pv[head] = pv[head] * shrink + out_v
                mixed[head] = mixed[head] * shrink + out_m
            return 0

        lax.fori_loop(heads[0], heads[-1] + 1, one_head, 0)

    early, every = 2 * PART, range(HEADS)
    mine, near, far = [(0, 0, TOK)], [(1, 0, early), (2, 0, early)], [(3, 0, early), (4, 0, early)]

    for copy in kv_sib:
        copy.wait_recv()
    kv_near = len(kv_sib)
    project(0, (z // 4, 2 + z // 4))
    w_far_end("key")
    w_far_end("value")
    for copy in kv_sib[kv_near:]:
        copy.wait_recv()
    project(0, (1 - z // 4, 3 - z // 4), False)
    kv_start(0)
    q_turn(0, 0)
    x_second(1)
    x_own(2)
    q_turn(0, 1)
    q_turn(1, 0)
    q_pass(2, 0)
    q_turn(0, 2)
    x_last(1)
    project(1)
    kv_start(1)
    q_turn(0, 3)
    q_turn(1, 1)
    q_turn(2, 0)
    x_first(2)
    q_turn(0, 4)
    q_turn(1, 2)
    kv_pass(0)
    q_turn(0, 5)
    q_turn(2, 1)
    q_turn(1, 3)
    q_turn(2, 2)
    q_turn(1, 4)
    x_second(2)
    kv_pass(1)
    q_turn(2, 3)
    q_turn(1, 5)
    q_sib[0].wait_recv()
    ask(0, (0, 1))
    x_last(2)
    project(2)
    kv_start(2)
    ask(0, (2,))
    q_turn(2, 4)
    kv_end(0)
    attend([0], mine, True)
    q_turn(2, 5)
    fr_copies[2].wait_recv()
    fr_copies[3].wait_recv()
    arrived(siba, 0)
    arrived(siba, 1)
    attend([0], near)
    kv_end(1)
    q_sib[1].wait_recv()
    ask(1)
    attend([1], mine, True)
    kv_pass(2)
    attend([1], near)
    q_sib[2].wait_recv()
    ask(2)
    attend([2], mine, True)
    attend([2], near)
    arrived(sibb, 0)
    arrived(sibb, 1)
    attend(every, far)
    arrived(siba, 2)
    attend(every, [(1, early, PART), (2, early, PART)])
    kv_end(2)
    attend(every, [(4, early, PART)])
    arrived(sibb, 2)
    attend(every, [(3, early, PART)], last=True)

    assert len(used) == N_REMOTE
    for copy in used:
        if not any(copy is other for other in sent):
            copy.wait_send()


def per_device(tokens, tangents, positions, frames, w_query, w_key, w_value):
    out = jax.ShapeDtypeStruct((TOK, COLS), jnp.bfloat16)
    vmem = pl.BlockSpec(memory_space=pltpu.VMEM)
    anywhere = pl.BlockSpec(memory_space=pl.ANY)
    bf16, f32 = jnp.bfloat16, jnp.float32
    return pl.pallas_call(
        kernel,
        out_shape=(out, out),
        in_specs=[vmem, vmem] + [anywhere] * 5,
        out_specs=(vmem, vmem),
        scratch_shapes=[
            pltpu.VMEM((PARTS, 4, 2 * PART, 2 * FEAT), bf16),
            pltpu.VMEM((4, 8 * DEPTH, 2 * COLS), bf16),
            pltpu.VMEM((HEADS, CTX // 2, 2, DEPTH, DH), bf16),
            pltpu.VMEM((SPAN + 1, 2, TOK, 2 * COLS), bf16),
            pltpu.VMEM((TOK, 2 * COLS), bf16),
            pltpu.VMEM((SPAN + 1, 8, TOK), jnp.int32),
            pltpu.VMEM((TOK, 128), jnp.int32),
            pltpu.VMEM((2 * PART, 2 * COLS), f32),
            pltpu.VMEM((HEADS, TOK, 128), f32),
            pltpu.VMEM((HEADS, TOK, 128), f32),
            pltpu.VMEM((HEADS, TOK, 128), f32),
            pltpu.VMEM((HEADS, TOK, 256), f32),
            pltpu.VMEM((HEADS, TOK, 128), f32),
            pltpu.SemaphoreType.DMA((2 + HEADS + 2 * PARTS,)),
            pltpu.SemaphoreType.DMA((N_REMOTE,)),
            pltpu.SemaphoreType.DMA((N_REMOTE,)),
        ],
        compiler_params=pltpu.CompilerParams(
            collective_id=0, has_side_effects=True, vmem_limit_bytes=56 << 20
        ),
        cost_estimate=pl.CostEstimate(flops=12_500_000_000, bytes_accessed=4_000_000, transcendentals=2_300_000),
        name="fused_attention",
    )(
        positions, frames.reshape(-1, 128), tokens, tangents, w_query, w_key, w_value
    )


def solution(mesh):
    return jax.shard_map(
        per_device,
        mesh=mesh,
        in_specs=(
            P("ctx", "fsdp"),
            P("ctx", "fsdp"),
            P("ctx"),
            P(),
            P("ctx", "fsdp"),
            P("ctx", "fsdp"),
            P("ctx", "fsdp"),
        ),
        out_specs=(P("ctx", "fsdp"), P("ctx", "fsdp")),
        check_vma=False,
    )
```

time: 130 us -> 124 us (0.954)
  Pallas kernels: 125 us -> 121 us
    pallas_call x1, Pallas kernels: 125 us -> 121 us  [per_device(): pl.pallas_call(kernel, out_shape=(out, out), in_specs=[vmem, vmem] + [any...]
where the time goes in v3:
time: 124 us
  Pallas kernels  121 us (98%)
  local copies, waits for them, and re-layouts  2.47 us (2%)
    pallas_call x1, Pallas kernels, per_device(): pl.pallas_call(kernel, out_shape=(out, out), in_specs=[vmem, vmem] + [any...  121 us

profile of v3, /device:TPU:1, one launch (start us, length us, event | category | flops | bytes accessed | tf_op | source)
XLA Modules:
  0.0 123.9 jit_solution(4015535429827838092)
XLA Ops:
  0.6 120.7 %fused_attention.1 = (bf16[384,384]{1,0:T(8,128)(2,1)}, bf16[384,384]{1,0:T(8,128)(2,1)}) custom-call(s32[384]{0:T(512)} %pos_ref.1, s32[96,128]{1,0:T(8,128)} %bitcast.1, bf16[384,640]{1,0:T(8,128)(2,1)} %tok_ref.1, bf16[384,640]{1,0:T(8,128)(2,1)} %tan_ref.1, bf16[160,384]{1,0:T(8,128)(2,1)} %wq_ref.1, bf16[160,384]{1,0:T(8,128)(2,1)} %wk_ref.1, ...), custom_call_target="tpu_custom_call" | custom-call | flops 12499999744 | bytes 4000000 | tf_op jit(solution)/shard_map/fused_attention/pallas_call | solution.py:482
  121.4 0.0 copy-start
  121.4 1.7 %copy.11 = bf16[384,384]{1,0:T(8,128)(2,1)} copy(bf16[384,384]{1,0:T(8,128)(2,1)} %get-tuple-element.4) | data formatting | bytes 589824
  123.1 0.0 copy-done
  123.2 0.7 copy.12
Async XLA Ops:
  121.4 1.8 %copy-start = (bf16[384,384]{1,0:T(8,128)(2,1)S(1)}, bf16[384,384]{1,0:T(8,128)(2,1)}, u32[]{:S(2)}) copy-start(bf16[384,384]{1,0:T(8,128)(2,1)} %get-tuple-element.5) | copy-start | bytes 884740

commit v4 on v3

--- a/solution.py
+++ b/solution.py
@@ -242,9 +242,9 @@
     w_swapped("key")
     w_turn("value", "own", 0)
     w_swapped("value")
+    x_first(0)
     x_here(1)
     x_swap(1)
-    x_first(0)
     for head in range(HEADS):
         loads[2 + head].wait()
         q_swap[head] = same(q_share(head, "own", 0), beside)

time: 124 us -> 124 us (level)
  no operation moved by 1% of the time
where the time goes in v4:
time: 124 us
  Pallas kernels  121 us (98%)
  local copies, waits for them, and re-layouts  2.47 us (2%)
    pallas_call x1, Pallas kernels, per_device(): pl.pallas_call(kernel, out_shape=(out, out), in_specs=[vmem, vmem] + [any...  121 us

profile of v4, /device:TPU:1, one launch (start us, length us, event | category | flops | bytes accessed | tf_op | source)
XLA Modules:
  0.0 123.9 jit_solution(46700270103673121)
XLA Ops:
  0.6 120.7 %fused_attention.1 = (bf16[384,384]{1,0:T(8,128)(2,1)}, bf16[384,384]{1,0:T(8,128)(2,1)}) custom-call(s32[384]{0:T(512)} %pos_ref.1, s32[96,128]{1,0:T(8,128)} %bitcast.1, bf16[384,640]{1,0:T(8,128)(2,1)} %tok_ref.1, bf16[384,640]{1,0:T(8,128)(2,1)} %tan_ref.1, bf16[160,384]{1,0:T(8,128)(2,1)} %wq_ref.1, bf16[160,384]{1,0:T(8,128)(2,1)} %wk_ref.1, ...), custom_call_target="tpu_custom_call" | custom-call | flops 12499999744 | bytes 4000000 | tf_op jit(solution)/shard_map/fused_attention/pallas_call | solution.py:482
  121.4 0.0 copy-start
  121.4 1.7 %copy.11 = bf16[384,384]{1,0:T(8,128)(2,1)} copy(bf16[384,384]{1,0:T(8,128)(2,1)} %get-tuple-element.4) | data formatting | bytes 589824
  123.1 0.0 copy-done
  123.1 0.7 copy.12
Async XLA Ops:
  121.4 1.8 %copy-start = (bf16[384,384]{1,0:T(8,128)(2,1)S(1)}, bf16[384,384]{1,0:T(8,128)(2,1)}, u32[]{:S(2)}) copy-start(bf16[384,384]{1,0:T(8,128)(2,1)} %get-tuple-element.5) | copy-start | bytes 884740
